TPU v7x, 32 devices: a whole 2x2x4 slice. The times are simulated.
32 devices in a mesh: seq: 4 (over y, x), tile: 8 (over z, core).
Axes of the slice: x: 2, y: 2, z: 4, core: 2. Of those that a mesh axis runs over, the one named last changes fastest.
Arguments:
- states: int32 [512, 384], P('seq'), may hold values from 0 to 20
- tile_blocks: int32 [8, 2], P('tile'), may hold values from 0 to 3, as said below
- couplings: bfloat16 [8, 2016, 2016], P('tile'), may hold values from -0.875 to 0.875
- fields: float32 [8064], P('tile'), may hold values from -8 to 305
Outputs:
- probs: bfloat16 [512, 8064], P('seq', 'tile')
- grad_couplings: float32 [8, 2016, 2016], P('tile', 'seq')
Inputs may be any that keep to these rules, and one draw needn't show every extreme that they name: `tile_blocks`: every tile names two blocks; each block is named by exactly three tiles: one naming it twice and two that pair it with another block; no unordered pair of blocks is named by two tiles.
All inputs are finite; a program needn't handle non-finite values.
Results may differ from a plain program's by a relative error of at most 0.023.
Values may be sent and summed in bfloat16 or wider, within the bound.
A program may use at most 128 MiB of HBM per device.

v0:
```python
import math

import jax
import jax.numpy as jnp
from jax import lax
from jax.sharding import PartitionSpec as P

Q = 21
LB = 96


def state_table(block_states):
    state_codes = jnp.arange(Q, dtype=jnp.int32)
    matches = block_states[:, :, None] == state_codes[None, None, :]
    return matches.astype(jnp.bfloat16).reshape(block_states.shape[0], block_states.shape[1] * Q)


def normalize(logits):
    row_total = logits.shape[0]
    shaped = logits.reshape(row_total, -1, Q)
    row_max = jnp.max(shaped, axis=2, keepdims=True)
    exponent = jnp.exp(shaped - row_max)
    result = exponent / jnp.sum(exponent, axis=2, keepdims=True)
    return result.astype(jnp.bfloat16).reshape(row_total, -1)


def body(states, tile_blocks, couplings, fields):
    row_total = states.shape[0]
    block_width = LB * Q
    total_width = states.shape[1] * Q
    lead_block = tile_blocks[0, 0]
    tail_block = tile_blocks[0, 1]
    residue = jnp.arange(block_width, dtype=jnp.int32) // Q
    keep_mask = jnp.logical_or(lead_block != tail_block, residue[:, None] != residue[None, :])
    masked = jnp.where(keep_mask, couplings[0], jnp.zeros((), jnp.bfloat16))
    lead_states = lax.dynamic_slice_in_dim(states, lead_block * LB, LB, 1)
    tail_states = lax.dynamic_slice_in_dim(states, tail_block * LB, LB, 1)
    lead_table = state_table(lead_states)
    tail_table = state_table(tail_states)
    to_lead = lax.dot_general(
        tail_table, masked, (((1,), (1,)), ((), ())), preferred_element_type=jnp.float32
    )
    to_tail = jnp.dot(lead_table, masked, preferred_element_type=jnp.float32)
    empty_buffer = jnp.zeros((row_total, total_width), jnp.float32)
    partial_value = lax.dynamic_update_slice_in_dim(
        empty_buffer, to_lead, lead_block * block_width, 1
    )
    partial_value = partial_value + lax.dynamic_update_slice_in_dim(
        empty_buffer, to_tail, tail_block * block_width, 1
    )
    owner_fields = lax.psum_scatter(
        partial_value.astype(jnp.bfloat16), "tile", scatter_dimension=1, tiled=True
    ).astype(jnp.float32)
    owner_probs = normalize(owner_fields + fields[None, :])
    all_probs = lax.all_gather(owner_probs, "tile", axis=1, tiled=True)
    lead_probs = lax.dynamic_slice_in_dim(all_probs, lead_block * block_width, block_width, 1)
    tail_probs = lax.dynamic_slice_in_dim(all_probs, tail_block * block_width, block_width, 1)
    lead_gap = (lead_probs.astype(jnp.float32) - lead_table.astype(jnp.float32)).astype(
        jnp.bfloat16
    )
    tail_gap = (tail_probs.astype(jnp.float32) - tail_table.astype(jnp.float32)).astype(
        jnp.bfloat16
    )
    grad_term = lax.dot_general(
        lead_gap, tail_table, (((0,), (0,)), ((), ())), preferred_element_type=jnp.float32
    )
    grad_term = grad_term + lax.dot_general(
        lead_table, tail_gap, (((0,), (0,)), ((), ())), preferred_element_type=jnp.float32
    )
    grad_scale = Q / math.sqrt(row_total * lax.axis_size("seq"))
    grad_term = jnp.where(keep_mask, grad_term * grad_scale, jnp.zeros((), jnp.float32))
    grad_share = lax.psum_scatter(
        grad_term[None, :, :].astype(jnp.bfloat16), "seq", scatter_dimension=1, tiled=True
    ).astype(jnp.float32)
    return (owner_probs, grad_share)


def solution(mesh):
    in_specs = (P("seq", None), P("tile", None), P("tile", None, None), P("tile"))
    out_specs = (P("seq", "tile"), P("tile", "seq", None))
    return jax.shard_map(body, mesh=mesh, in_specs=in_specs, out_specs=out_specs, check_vma=False)
```

profile of v0, /device:TPU:28, one launch (start us, length us, event | category | flops | bytes accessed | tf_op | source)
XLA Modules:
  0.0 202.6 jit_solution(15993021763827336652)
XLA Ops:
  7.2 0.0 reduce-scatter.6.cloned.1.call-start
  7.2 1.3 fusion.21
  12.4 1.1 constant_dynamic-slice_fusion
  13.5 0.1 copy.11
  13.6 0.1 copy.10
  13.7 0.2 iota_compare_fusion.1
  13.9 0.2 eq.71
  14.1 0.2 iota_compare_fusion
  14.3 0.2 eq.75
  14.6 0.3 broadcast_in_dim.9
  14.9 6.5 %convolution_dynamic-update-slice_fusion = f32[128,8064]{0,1:T(8,128)S(1)} fusion(f32[128,8064]{0,1:T(8,128)S(1)} %broadcast_in_dim.9, s32[]{:T(128)S(6)} %select_n.45, pred[128,2016]{0,1:T(32,128)(4,1)S(1)} %eq.71, bf16[1,2016,2016]{2,1,0:T(8,128)(2,1)} %param.6, s32[2016]{0:T(1024)S(1)} %add_select_fusion, pred[]{:T(512)} %bitcast.1), kind=kOutput, calls=%fused_computation.5 | convolution fusion | flops 1052642304 | bytes 9435141 | tf_op jit(solution)/shard_map/dot_general | solution.py:40
  21.4 4.9 %fusion.3 = f32[128,8064]{0,1:T(8,128)S(1)} fusion(f32[128,8064]{0,1:T(8,128)S(1)} %convolution_dynamic-update-slice_fusion, s32[]{:T(128)S(6)} %select_n.46, pred[128,2016]{0,1:T(32,128)(4,1)S(1)} %eq.75, bf16[1,2016,2016]{2,1,0:T(8,128)(2,1)S(1)} %bitcast.33, s32[2016]{0:T(1024)S(1)} %add_select_fusion, pred[]{:T(512)} %bitcast.1), kind=kOutput, calls=%fused_computation.7 | convolution fusion | flops 1052900352 | bytes 10596357 | tf_op jit(solution)/shard_map/dot_general | solution.py:43
  26.3 1.5 convert_element_type.45
  27.8 0.0 reduce-scatter.6.cloned.1.call-update
  27.8 0.0 all-gather.2.cloned.1.call-start
  27.9 32.9 %reduce-scatter.6.cloned.1.call-done = bf16[128,1008]{0,1:T(8,128)(2,1)} async-done(((bf16[128,8064]{0,1:T(8,128)(2,1)}), bf16[128,1008]{0,1:T(8,128)(2,1)}) %reduce-scatter.6.cloned.1.call-update) | async-done | bytes 258064 | tf_op jit(solution)/shard_map/reduce_scatter | solution.py:51
  60.8 1.2 convert_add_fusion
  62.1 0.1 reduce_max.9
  62.2 1.3 fusion
  63.7 0.9 divide_convert_fusion
  64.6 0.2 reduce-scatter.8.cloned.1.call-start
  64.9 0.2 eq.78
  65.0 0.1 eq.72
  65.1 0.1 eq.76
  65.2 0.1 eq.68
  65.3 0.1 eq.81
  65.4 0.3 broadcast_compare_fusion.1
  65.7 28.8 %all-gather.2.cloned.1.call-done = bf16[128,8064]{0,1:T(8,128)(2,1)} async-done(((bf16[128,1008]{0,1:T(8,128)(2,1)}), bf16[128,8064]{0,1:T(8,128)(2,1)}) %all-gather.2.cloned.1.call-update) | async-done | bytes 2064400 | tf_op jit(solution)/shard_map/all_gather | solution.py:55
  94.5 3.4 %fusion.8 = f32[2016,2016]{1,0:T(8,128)S(1)} fusion(pred[128,2016]{0,1:T(32,128)(4,1)S(1)} %get-tuple-element.5, pred[128,2016]{0,1:T(32,128)(4,1)S(1)} %get-tuple-element.4, bf16[128,8064]{0,1:T(8,128)(2,1)} %all-gather.2.cloned.1.call-done, s32[]{:T(128)S(6)} %select_n.45), kind=kOutput, calls=%fused_computation.15 | convolution fusion | flops 1041739776 | bytes 17289220 | tf_op jit(solution)/shard_map/dot_general | solution.py:64
  97.9 7.7 %fusion.2 = bf16[1,2016,2016]{2,1,0:T(8,128)(2,1)} fusion(f32[2016,2016]{1,0:T(8,128)S(1)} %fusion.8, pred[128,2016]{0,1:T(32,128)(4,1)S(1)} %get-tuple-element.4, s32[2016]{0:T(1024)S(1)} %add_select_fusion, pred[]{:T(512)} %bitcast.1, pred[128,2016]{0,1:T(32,128)(4,1)S(1)} %get-tuple-element.5, bf16[128,8064]{0,1:T(8,128)(2,1)} %all-gather.2.cloned.1.call-done, ...), kind=kOutput, calls=%fused_computation.4 | convolution fusion | flops 1066125312 | bytes 25692676 | tf_op jit(solution)/shard_map/dot_general | solution.py:67
  105.6 86.3 %reduce-scatter.8.cloned.1.call-done = bf16[1,504,2016]{2,1,0:T(8,128)(2,1)} async-done(((bf16[1,2016,2016]{2,1,0:T(8,128)(2,1)}), bf16[1,504,2016]{2,1,0:T(8,128)(2,1)}) %reduce-scatter.8.cloned.1.call-update) | async-done | bytes 2032144
  191.9 4.1 %convert_element_type.58 = f32[1,504,2016]{2,1,0:T(8,128)} convert(bf16[1,504,2016]{2,1,0:T(8,128)(2,1)} %reduce-scatter.8.cloned.1.call-done) | non-fusion elementwise | flops 1016064 | bytes 6096384 | tf_op jit(solution)/shard_map/convert_element_type | solution.py:74
  (17 shorter events, 0.2 us)
Async XLA Ops:
  7.2 53.7 %reduce-scatter.6.cloned.1.call-start = ((), (), s32[]{:S(2)}) async-start(), calls=%async_computation.2 | async-start | bytes 2322432 | tf_op jit(solution)/shard_map/reduce_scatter | solution.py:51
  14.6 6.8 %slice-start = ((s8[8257536]{0:T(1024)(128)(4,1)}), s8[4194304]{0:T(1024)(128)(4,1)S(1)}, s32[]{:S(2)}) async-start(s8[8257536]{0:T(1024)(128)(4,1)} %bitcast.32), calls=%async_computation.5 | async-start | bytes 8388608
  14.9 6.5 %slice-start.1 = ((s8[8257536]{0:T(1024)(128)(4,1)}), s8[4063232]{0:T(1024)(128)(4,1)S(1)}, s32[]{:S(2)}) async-start(s8[8257536]{0:T(1024)(128)(4,1)} %bitcast.32), calls=%async_computation.6 | async-start | bytes 8126464
  26.3 34.5 %copy-start.1 = (f32[1008]{0:T(1024)S(1)}, f32[1008]{0:T(1024)}, u32[]{:S(2)}) copy-start(f32[1008]{0:T(1024)} %param.7) | copy-start | bytes 12100
  27.8 66.7 %all-gather.2.cloned.1.call-start = ((), (), s32[]{:S(2)}) async-start(), calls=%async_computation.3 | async-start | bytes 2322432 | tf_op jit(solution)/shard_map/all_gather | solution.py:55
  60.8 2.8 %copy-start = (bf16[128,1008]{0,1:T(8,128)(2,1)S(1)}, bf16[128,1008]{0,1:T(8,128)(2,1)}, u32[]{:S(2)}) copy-start(bf16[128,1008]{0,1:T(8,128)(2,1)} %reduce-scatter.6.cloned.1.call-done) | copy-start | bytes 774148
  64.6 127.3 %reduce-scatter.8.cloned.1.call-start = ((), (), s32[]{:S(2)}) async-start(), calls=%async_computation.4 | async-start | bytes 10321920
Sparse Core Ops, SparseCore 0:
  28.0 32.8 reduce-scatter.5
  64.7 29.7 all-gather.1
  105.7 86.1 reduce-scatter.7
where the time goes:
time: 205 us; the launch traced here: 203 us
  waiting for transfers between devices  148 us (72%)
  matrix products  22.5 us (11%)
  between operations  17.9 us (9%)
  other arithmetic  9.86 us (5%)
  local copies, waits for them, and re-layouts  3.93 us (2%)
    unnamed x4, waiting for transfers between devices  86.4 us
    reduce_scatter x1, waiting for transfers between devices, body(): lax.psum_scatter(partial_value.astype(jnp.bfloat16), 'tile', scatter_dime...  32.9 us
    all_gather x1, waiting for transfers between devices, body(): all_probs = lax.all_gather(owner_probs, 'tile', axis=1, tiled=True)  28.8 us
    dot_general x1, matrix products, body(): lax.dot_general(lead_table, tail_gap, (((0,), (0,)), ((), ())), preferred...  7.7 us
    dot_general x1, matrix products, body(): lax.dot_general(tail_table, masked, (((1,), (1,)), ((), ())), preferred_e...  6.49 us
    dot_general x1, matrix products, body(): to_tail = jnp.dot(lead_table, masked, preferred_element_type=jnp.float32)  4.89 us
  transfers between devices with their start and end apart: 3, of which 3 were waited for; matrix products, arithmetic and copies ran while one was open for 0% of the time, Pallas kernels for 0%

commit v1 on v0

v1 whole, which is shorter than its diff:
```python
import functools
import math

import jax
import jax.numpy as jnp
from jax import lax
from jax.experimental import pallas as pl
from jax.experimental.pallas import tpu as pltpu
from jax.sharding import PartitionSpec as P

Q = 21
LB = 96
WIDTH = LB * Q
HALF = WIDTH // 2
CHUNKS = 4


def state_table(block_states):
    state_codes = jnp.arange(Q, dtype=jnp.int32)
    matches = block_states[:, :, None] == state_codes[None, None, :]
    return matches.astype(jnp.bfloat16).reshape(block_states.shape[0], block_states.shape[1] * Q)


def normalize(logits):
    row_total = logits.shape[0]
    shaped = logits.reshape(row_total, -1, Q)
    row_max = jnp.max(shaped, axis=2, keepdims=True)
    exponent = jnp.exp(shaped - row_max)
    result = exponent / jnp.sum(exponent, axis=2, keepdims=True)
    return result.astype(jnp.bfloat16).reshape(row_total, -1)


def send(src, dst, send_sem, recv_sem, **device):
    return pltpu.make_async_remote_copy(
        src_ref=src,
        dst_ref=dst,
        send_sem=send_sem,
        recv_sem=recv_sem,
        device_id=device,
        device_id_type=pl.DeviceIdType.MESH,
    )


def greet(groups, seqs):
    tile = lax.axis_index("tile")
    group, core = tile // 2, tile % 2
    seq = lax.axis_index("seq")
    barrier = pltpu.get_barrier_semaphore()
    mesh_id = pl.DeviceIdType.MESH
    pl.semaphore_signal(
        barrier, inc=1, device_id={"tile": group * 2 + 1 - core}, device_id_type=mesh_id
    )
    for k in range(1, groups):
        pl.semaphore_signal(
            barrier,
            inc=1,
            device_id={"tile": ((group + k) % groups) * 2 + core},
            device_id_type=mesh_id,
        )
    for k in range(1, seqs):
        pl.semaphore_signal(
            barrier, inc=1, device_id={"seq": (seq + k) % seqs}, device_id_type=mesh_id
        )
    pl.semaphore_wait(barrier, groups + max(seqs - 1, 0))


def reduce_kernel(
    groups, blocks, lead, tail, out, halves, mine, stage, mate_in, onward, arrived, sems
):
    tile = lax.axis_index("tile")
    group, core = tile // 2, tile % 2
    mate = group * 2 + 1 - core
    lead_block, tail_block = blocks[0, 0], blocks[0, 1]
    for h in range(2):
        halves[0, h] = lead[:, h * HALF : (h + 1) * HALF]
        halves[1, h] = tail[:, h * HALF : (h + 1) * HALF]

    def part(g, h):
        in_lead = (lead_block == g).astype(jnp.float32)
        in_tail = (tail_block == g).astype(jnp.float32)
        return (halves[0, h] * in_lead + halves[1, h] * in_tail).astype(jnp.bfloat16)

    greet(groups, 0)

    def to_mate(k):
        return send(stage.at[k], mate_in.at[k], sems.at[0, k], sems.at[1, k], tile=mate)

    def to_owner(k):
        owner = ((group + k) % groups) * 2 + core
        return send(onward.at[k], arrived.at[k], sems.at[2, k], sems.at[3, k], tile=owner)

    def first(k, carry):
        k = (k + 1) % groups
        stage[k] = part((group + k) % groups, 1 - core)
        to_mate(k).start()
        return carry

    lax.fori_loop(0, groups, first, 0)

    def second(k, carry):
        mine[...] = part((group + k) % groups, core).astype(jnp.float32)
        to_mate(k).wait_recv()
        onward[k] = (mine[...] + mate_in[k].astype(jnp.float32)).astype(jnp.bfloat16)
        to_owner(k).start()
        return carry

    lax.fori_loop(1, groups, second, 0)
    to_mate(0).wait_recv()
    mine[...] = part(group, core).astype(jnp.float32) + mate_in[0].astype(jnp.float32)

    def third(k, carry):
        to_owner(k).wait()
        mine[...] += arrived[k].astype(jnp.float32)
        return carry

    lax.fori_loop(1, groups, third, 0)

    def fourth(k, carry):
        to_mate(k).wait_send()
        return carry

    lax.fori_loop(0, groups, fourth, 0)
    out[...] = mine[...]


def exchange_kernel(groups, seqs, blocks, probs, tails, leads, *scratch):
    every = scratch[:CHUNKS]
    tail_out = scratch[CHUNKS : 2 * CHUNKS]
    lead_out, near, pair, over = scratch[2 * CHUNKS :]
    tile = lax.axis_index("tile")
    group, core = tile // 2, tile % 2
    seq = lax.axis_index("seq")
    mate = group * 2 + 1 - core
    lead_block, tail_block = blocks[0, 0], blocks[0, 1]
    rows = probs.shape[0] // CHUNKS
    share = WIDTH // seqs
    greet(groups, seqs)

    def to_group(c, k):
        other = ((group + k) % groups) * 2 + core
        mine = every[c].at[group, core]
        return send(mine, mine, near.at[0, c, k], near.at[1, c, k], tile=other)

    def to_mate(c, k):
        block = every[c].at[(group + groups - k) % groups, core]
        return send(block, block, pair.at[0, c, k], pair.at[1, c, k], tile=mate)

    def tail_to(c, k):
        place = tails.at[seq, pl.ds(c * rows, rows)]
        return send(tail_out[c], place, over.at[0, c, k], over.at[1, c, k], seq=(seq + k) % seqs)

    def lead_to(c, k):
        other = (seq + k) % seqs
        place = leads.at[seq, pl.ds(c * rows, rows)]
        return send(
            lead_out.at[c, other], place, over.at[2, c, k], over.at[3, c, k], seq=other
        )

    for c in range(CHUNKS):
        every[c][group, core] = probs[c * rows : (c + 1) * rows]

        def start_far(k, carry, c=c):
            to_group(c, k).start()
            return carry

        lax.fori_loop(1, groups, start_far, 0)
        to_mate(c, 0).start()

    for c in range(CHUNKS):

        def relay(k, carry, c=c):
            to_group(c, k).wait_recv()
            to_mate(c, k).start()
            return carry

        lax.fori_loop(1, groups, relay, 0)

        def gathered(k, carry, c=c):
            to_mate(c, k).wait_recv()
            return carry

        lax.fori_loop(0, groups, gathered, 0)
        for h in range(2):
            tail_out[c][:, h * HALF : (h + 1) * HALF] = every[c][tail_block, h]
            block_half = every[c][lead_block, h]
            for j in range(seqs // 2):
                lead_out[c, h * (seqs // 2) + j] = block_half[:, j * share : (j + 1) * share]

        def start_over(k, carry, c=c):
            tail_to(c, k).start()
            lead_to(c, k).start()
            return carry

        lax.fori_loop(1, seqs, start_over, 0)
        tails[seq, c * rows : (c + 1) * rows] = tail_out[c][...]
        leads[seq, c * rows : (c + 1) * rows] = lead_out[c, seq]

    for c in range(CHUNKS):

        def finish(k, carry, c=c):
            tail_to(c, k).wait()
            lead_to(c, k).wait()
            return carry

        lax.fori_loop(1, seqs, finish, 0)

        def sent_far(k, carry, c=c):
            to_group(c, k).wait_send()
            return carry

        lax.fori_loop(1, groups, sent_far, 0)

        def sent_pair(k, carry, c=c):
            to_mate(c, k).wait_send()
            return carry

        lax.fori_loop(0, groups, sent_pair, 0)


def reduce_fields(tile_blocks, lead, tail, groups):
    rows = lead.shape[0]
    slots = pltpu.VMEM((groups, rows, HALF), jnp.bfloat16)
    vmem = pl.BlockSpec(memory_space=pltpu.VMEM)
    return pl.pallas_call(
        functools.partial(reduce_kernel, groups),
        out_shape=jax.ShapeDtypeStruct((rows, HALF), jnp.float32),
        in_specs=[pl.BlockSpec(memory_space=pltpu.SMEM), vmem, vmem],
        out_specs=vmem,
        scratch_shapes=[
            pltpu.VMEM((2, 2, rows, HALF), jnp.float32),
            pltpu.VMEM((rows, HALF), jnp.float32),
            slots,
            slots,
            slots,
            slots,
            pltpu.SemaphoreType.DMA((4, groups)),
        ],
        compiler_params=pltpu.CompilerParams(
            collective_id=0, has_side_effects=True, vmem_limit_bytes=48 << 20
        ),
    )(tile_blocks, lead, tail)


def exchange(tile_blocks, probs, groups, seqs):
    rows = probs.shape[0]
    part = rows // CHUNKS
    vmem = pl.BlockSpec(memory_space=pltpu.VMEM)
    return pl.pallas_call(
        functools.partial(exchange_kernel, groups, seqs),
        out_shape=[
            jax.ShapeDtypeStruct((seqs, rows, WIDTH), jnp.bfloat16),
            jax.ShapeDtypeStruct((seqs, rows, WIDTH // seqs), jnp.bfloat16),
        ],
        in_specs=[pl.BlockSpec(memory_space=pltpu.SMEM), vmem],
        out_specs=[vmem, vmem],
        scratch_shapes=[pltpu.VMEM((groups, 2, part, HALF), jnp.bfloat16)] * CHUNKS
        + [pltpu.VMEM((part, WIDTH), jnp.bfloat16)] * CHUNKS
        + [
            pltpu.VMEM((CHUNKS, seqs, part, WIDTH // seqs), jnp.bfloat16),
            pltpu.SemaphoreType.DMA((2, CHUNKS, groups)),
            pltpu.SemaphoreType.DMA((2, CHUNKS, groups)),
            pltpu.SemaphoreType.DMA((4, CHUNKS, seqs)),
        ],
        compiler_params=pltpu.CompilerParams(
            collective_id=1, has_side_effects=True, vmem_limit_bytes=48 << 20
        ),
    )(tile_blocks, probs)


def body(states, tile_blocks, couplings, fields):
    groups = lax.axis_size("tile") // 2
    seqs = lax.axis_size("seq")
    seq = lax.axis_index("seq")
    row_total = states.shape[0] * seqs
    share = WIDTH // seqs
    lead_block = tile_blocks[0, 0]
    tail_block = tile_blocks[0, 1]
    apart = lead_block != tail_block
    residue = jnp.arange(WIDTH, dtype=jnp.int32) // Q
    keep_mask = jnp.logical_or(apart, residue[:, None] != residue[None, :])
    masked = jnp.where(keep_mask, couplings[0], jnp.zeros((), jnp.bfloat16))
    lead_states = lax.dynamic_slice_in_dim(states, lead_block * LB, LB, 1)
    tail_states = lax.dynamic_slice_in_dim(states, tail_block * LB, LB, 1)
    both_states = lax.all_gather(
        jnp.concatenate([lead_states, tail_states], axis=1), "seq", axis=0, tiled=True
    )
    lead = lax.dot_general(
        state_table(tail_states),
        masked,
        (((1,), (1,)), ((), ())),
        preferred_element_type=jnp.float32,
    )
    tail = jnp.dot(state_table(lead_states), masked, preferred_element_type=jnp.float32)
    logits = reduce_fields(tile_blocks, lead, tail, groups)
    probs = normalize(logits + fields[None, :])
    tail_probs, lead_probs = exchange(tile_blocks, probs, groups, seqs)
    tail_probs = tail_probs.reshape(row_total, WIDTH)
    lead_probs = lead_probs.reshape(row_total, share)
    share_states = lax.dynamic_slice_in_dim(both_states, seq * (LB // seqs), LB // seqs, 1)
    lead_table = state_table(share_states)
    tail_table = state_table(both_states[:, LB:])
    lead_gap = lead_probs - lead_table
    tail_gap = tail_probs - tail_table
    grad = lax.dot_general(
        lead_gap, tail_table, (((0,), (0,)), ((), ())), preferred_element_type=jnp.float32
    )
    grad = grad + lax.dot_general(
        lead_table, tail_gap, (((0,), (0,)), ((), ())), preferred_element_type=jnp.float32
    )
    grad_scale = Q / math.sqrt(row_total)
    own_residue = seq * (LB // seqs) + jnp.arange(share, dtype=jnp.int32) // Q
    own_mask = jnp.logical_or(apart, own_residue[:, None] != residue[None, :])
    grad = jnp.where(own_mask, grad * grad_scale, jnp.zeros((), jnp.float32))
    return (probs, grad[None])


def solution(mesh):
    in_specs = (P("seq", None), P("tile", None), P("tile", None, None), P("tile"))
    out_specs = (P("seq", "tile"), P("tile", "seq", None))
    return jax.shard_map(body, mesh=mesh, in_specs=in_specs, out_specs=out_specs, check_vma=False)
```

time: 205 us -> 148 us (0.72)
  waiting for transfers between devices: 148 us -> 0 us
  Pallas kernels: 0 us -> 73.7 us
  local copies, waits for them, and re-layouts: 3.93 us -> 26.1 us
  between operations: 17.9 us -> 3.52 us
  blocking collectives: 0 us -> 11.8 us
    unnamed x4 -> x0, waiting for transfers between devices: 86.4 us -> none
    pallas_call x0 -> x2, Pallas kernels: none -> 73.7 us  [the longest x1 45.1 us: exchange(): pl.pallas_call(functools.partial(exchange_kernel, groups, seqs), out_shap...]
    reduce_scatter x1 -> x0, waiting for transfers between devices: 32.9 us -> none  [body(): lax.psum_scatter(partial_value.astype(jnp.bfloat16), 'tile', scatter_dime...]
    all_gather x1 -> x0, waiting for transfers between devices: 28.8 us -> none  [body(): all_probs = lax.all_gather(owner_probs, 'tile', axis=1, tiled=True)]
    eq x8 -> x14, local copies, waits for them, and re-layouts: 0.89 us -> 18.4 us  [state_table(): matches = block_states[:, :, None] == state_codes[None, None, :]]
    all_gather x0 -> x1, blocking collectives: none -> 11.8 us  [body(): lax.all_gather(jnp.concatenate([lead_states, tail_states], axis=1), 'seq'...]
    convert_element_type x2 -> x0, other arithmetic: 5.59 us -> none  [the longest x1 4.08 us: body(): grad_share = lax.psum_scatter(grad_term[None, :, :].astype(jnp.bfloat16),...]
    sub x0 -> x2, other arithmetic: none -> 5.23 us  [the longest x1 4.23 us: body(): tail_gap = tail_probs - tail_table]
  transfers between devices with their start and end apart: 3 -> 0, of which waited for: 3 -> 0; matrix products, arithmetic and copies ran while one was open for 0% -> 0% of each run, Pallas kernels for 0% -> 0%
where the time goes in v1:
time: 148 us; the launch traced here: 147 us
  Pallas kernels  73.7 us (50%)
  local copies, waits for them, and re-layouts  26.1 us (18%)
  matrix products  22.3 us (15%)
  blocking collectives  11.8 us (8%)
  other arithmetic  9.22 us (6%)
  between operations  3.52 us (2%)
    pallas_call x1, Pallas kernels, exchange(): pl.pallas_call(functools.partial(exchange_kernel, groups, seqs), out_shap...  45.1 us
    pallas_call x1, Pallas kernels, reduce_fields(): pl.pallas_call(functools.partial(reduce_kernel, groups), out_shape=jax.Sh...  28.6 us
    eq x14, local copies, waits for them, and re-layouts, state_table(): matches = block_states[:, :, None] == state_codes[None, None, :]  18.4 us
    all_gather x1, blocking collectives, body(): lax.all_gather(jnp.concatenate([lead_states, tail_states], axis=1), 'seq'...  11.8 us
    dot_general x1, matrix products, body(): jnp.dot(state_table(lead_states), masked, preferred_element_type=jnp.floa...  6 us
    dot_general x1, matrix products, body(): lax.dot_general(state_table(tail_states), masked, (((1,), (1,)), ((), ())...  5.84 us
    dot_general x1, matrix products, body(): lax.dot_general(lead_table, tail_gap, (((0,), (0,)), ((), ())), preferred...  5.75 us
    dot_general x1, matrix products, body(): lax.dot_general(lead_gap, tail_table, (((0,), (0,)), ((), ())), preferred...  4.67 us

profile of v1, /device:TPU:28, one launch (start us, length us, event | category | flops | bytes accessed | tf_op | source)
XLA Modules:
  0.0 146.6 jit_solution(2065777708512184282)
XLA Ops:
  0.6 1.3 fusion.21
  3.3 1.1 constant_dynamic-slice_fusion.1
  4.4 0.2 iota_compare_fusion.2
  4.6 0.2 eq.123
  6.2 6.0 %fusion.3.tail = f32[128,2016]{1,0:T(8,128)S(1)} fusion(pred[128,2016]{0,1:T(32,128)(4,1)S(1)} %eq.123, bf16[1,2016,2016]{2,1,0:T(8,128)(2,1)} %param.6, s32[2016]{0:T(1024)S(1)} %add_select_fusion, pred[]{:T(512)} %bitcast.1), kind=kOutput, calls=%fused_computation.7 | convolution fusion | flops 1052642304 | bytes 9426817 | tf_op jit(solution)/shard_map/dot_general | solution.py:293
  12.3 0.2 iota_compare_fusion.3
  12.5 0.2 eq.119
  12.7 5.8 %fusion.5.lead = f32[128,2016]{1,0:T(8,128)S(1)} fusion(bf16[1,2016,2016]{2,1,0:T(8,128)(2,1)} %param.6, s32[2016]{0:T(1024)S(1)} %add_select_fusion, pred[]{:T(512)} %bitcast.1, pred[128,2016]{0,1:T(32,128)(4,1)S(1)} %eq.119), kind=kOutput, calls=%fused_computation.8 | convolution fusion | flops 1052900352 | bytes 9426817 | tf_op jit(solution)/shard_map/dot_general | solution.py:287
  18.5 28.6 %shard_map.59 = f32[128,1008]{1,0:T(8,128)S(1)} custom-call(s32[1,2]{1,0:T(1,128)S(1)} %copy-done, f32[128,2016]{1,0:T(8,128)S(1)} %fusion.5.lead, f32[128,2016]{1,0:T(8,128)S(1)} %fusion.3.tail), custom_call_target="tpu_custom_call" | custom-call | tf_op jit(solution)/shard_map/pallas_call | solution.py:224
  47.2 0.2 copy.13
  47.6 1.3 fusion
  48.9 0.2 copy.15
  49.2 0.2 copy.14
  49.4 0.2 divide_convert_fusion.probs
  49.6 45.1 %shard_map.60 = (bf16[4,128,2016]{2,1,0:T(8,128)(2,1)S(1)}, bf16[4,128,504]{2,1,0:T(8,128)(2,1)S(1)}) custom-call(s32[1,2]{1,0:T(1,128)S(1)} %copy-done, bf16[128,1008]{1,0:T(8,128)(2,1)S(1)} %divide_convert_fusion.probs), custom_call_target="tpu_custom_call" | custom-call | tf_op jit(solution)/shard_map/pallas_call | solution.py:248
  94.9 11.8 %all_gather.3 = s32[512,192]{1,0:T(8,128)S(1)} all-gather(s32[128,192]{1,0:T(8,128)S(1)} %pad_add_fusion), channel_id=1, replica_groups=mesh['seq'=4,'tile'=8] {'seq'}, dimensions={0}, use_global_device_ids=true | all-gather | bytes 491520 | tf_op jit(solution)/shard_map/all_gather | solution.py:284
  106.7 0.8 slice.12
  107.5 1.8 %copy.18 = s32[512,96]{0,1:T(8,128)} copy(s32[512,96]{1,0:T(8,128)} %slice.12) | data formatting | bytes 393216 | tf_op jit(solution)/shard_map/slice | solution.py:301
  109.3 3.6 %eq.130 = s32[512,96,21]{0,2,1:T(8,128)} broadcast(s32[512,96]{0,1:T(8,128)} %copy.18), dimensions={0,1} | broadcast | bytes 4325376 | tf_op jit(solution)/shard_map/eq | solution.py:20
  112.9 5.8 %eq.137 = s32[4,128,2016]{1,0,2:T(4,128)} reshape(s32[512,96,21]{0,2,1:T(8,128)} %eq.130) | data formatting | bytes 8257536 | tf_op jit(solution)/shard_map/eq | solution.py:20
  118.7 5.3 %copy.19 = s32[4,128,2016]{2,1,0:T(8,128)} copy(s32[4,128,2016]{1,0,2:T(4,128)} %eq.137) | data formatting | bytes 8257536 | tf_op jit(solution)/shard_map/eq | solution.py:20
  124.1 4.2 %fusion.2 = bf16[4,128,2016]{2,1,0:T(8,128)(2,1)} fusion(bf16[4,128,2016]{2,1,0:T(8,128)(2,1)S(1)} %get-tuple-element.5, s32[4,128,2016]{2,1,0:T(8,128)} %copy.19, s32[2016]{0:T(1024)S(1)} %eq.139), kind=kLoop, calls=%fused_computation.6 | loop fusion | flops 3096576 | bytes 8265600 | tf_op jit(solution)/shard_map/sub | solution.py:303
  128.6 0.6 copy-done.2
  129.4 0.4 eq.125
  129.7 0.4 copy.17
  130.2 1.0 fusion.9
  131.2 1.7 %iota_compare_fusion = pred[512,96,21]{0,2,1:T(8,128)(4,1)S(1)} fusion(s32[512,96]{0,1:T(8,128)} %copy.18), kind=kLoop, calls=%fused_computation.3 | loop fusion | flops 1032192 | bytes 1228800 | tf_op jit(solution)/shard_map/eq | solution.py:20
  132.9 2.0 %eq.133 = pred[512,2016]{0,1:T(32,128)(4,1)} reshape(pred[512,96,21]{0,2,1:T(8,128)(4,1)S(1)} %iota_compare_fusion) | data formatting | bytes 2064384 | tf_op jit(solution)/shard_map/eq | solution.py:20
  134.9 4.7 %fusion.22 = f32[504,2016]{1,0:T(8,128)} fusion(bf16[512,504]{1,0:T(8,128)(2,1)} %bitcast.35, pred[512,2016]{0,1:T(32,128)(4,1)} %eq.133), kind=kOutput, calls=%fused_computation.43 | convolution fusion | flops 1040449536 | bytes 5612544 | tf_op jit(solution)/shard_map/dot_general | solution.py:304
  139.7 0.2 eq.136
  140.0 5.7 %select_bitcast_fusion = f32[1,504,2016]{2,1,0:T(8,128)} fusion(f32[504,2016]{1,0:T(8,128)} %fusion.22, pred[512,504]{0,1:T(8,128)(4,1)S(1)} %eq.136, bf16[512,2016]{1,0:T(8,128)(2,1)S(1)} %bitcast.34, s32[2016]{0:T(1024)S(1)} %add_select_fusion, s32[504]{0:T(512)S(1)} %fusion.15, pred[]{:T(512)} %bitcast.1), kind=kOutput, calls=%fused_computation.5 | convolution fusion | flops 1045529856 | bytes 10461025 | tf_op jit(solution)/shard_map/dot_general | solution.py:307
  145.7 0.9 copy.20
  (28 shorter events, 1.4 us)
Async XLA Ops:
  12.7 5.9 %copy-start = (s32[1,2]{1,0:T(1,128)S(1)}, s32[1,2]{1,0:T(1,128)}, u32[]{:S(2)}) copy-start(s32[1,2]{1,0:T(1,128)} %blocks.3) | copy-start | bytes 28
  12.7 34.5 %copy-start.4 = (f32[1008]{0:T(1024)S(1)}, f32[1008]{0:T(1024)}, u32[]{:S(2)}) copy-start(f32[1008]{0:T(1024)} %param.7) | copy-start | bytes 12100
  128.6 0.6 copy-start.2
  132.9 7.1 %copy-start.1 = (bf16[4,128,2016]{2,1,0:T(8,128)(2,1)S(1)}, bf16[4,128,2016]{2,1,0:T(8,128)(2,1)}, u32[]{:S(2)}) copy-start(bf16[4,128,2016]{2,1,0:T(8,128)(2,1)} %fusion.2) | copy-start | bytes 6193156
  134.9 4.7 %copy-start.3 = (s32[512,24]{0,1:T(8,128)S(1)}, s32[512,24]{0,1:T(8,128)}, u32[]{:S(2)}) copy-start(s32[512,24]{0,1:T(8,128)} %copy-done.2) | copy-start | bytes 147460

commit v2 on v1

--- a/solution.py
+++ b/solution.py
@@ -13,12 +13,24 @@
 WIDTH = LB * Q
 HALF = WIDTH // 2
 CHUNKS = 4
-
-
-def state_table(block_states):
-    state_codes = jnp.arange(Q, dtype=jnp.int32)
-    matches = block_states[:, :, None] == state_codes[None, None, :]
-    return matches.astype(jnp.bfloat16).reshape(block_states.shape[0], block_states.shape[1] * Q)
+ROW_TILE = WIDTH // 6
+COLUMN_TILE = 512
+
+
+def residue_of(index):
+    return (index * 3121) >> 16
+
+
+def table(states, first, columns):
+    lanes = states.shape[1]
+    residue = residue_of(lax.broadcasted_iota(jnp.int32, (lanes, columns), 1)) + first
+    place = lax.broadcasted_iota(jnp.int32, (lanes, columns), 0) == residue
+    spread = jnp.dot(
+        states, place.astype(jnp.float32).astype(jnp.bfloat16), preferred_element_type=jnp.float32
+    )
+    column = lax.broadcasted_iota(jnp.int32, (1, columns), 1)
+    code = (column - residue_of(column) * Q).astype(jnp.float32)
+    return jnp.where(spread == code, 1.0, 0.0)
 
 
 def normalize(logits):
@@ -28,6 +40,112 @@
     exponent = jnp.exp(shaped - row_max)
     result = exponent / jnp.sum(exponent, axis=2, keepdims=True)
     return result.astype(jnp.bfloat16).reshape(row_total, -1)
+
+
+def field_kernel(blocks, states, weights, lead, tail, tail_table):
+    step = pl.program_id(0)
+    rows, width = weights.shape[1], weights.shape[2]
+    first = step * (rows // Q)
+
+    @pl.when(step == 0)
+    def _():
+        tail_table[...] = table(states[:, 128:], 0, width).astype(jnp.bfloat16)
+        tail[...] = jnp.zeros_like(tail)
+
+    own = residue_of(lax.broadcasted_iota(jnp.int32, (rows, 1), 0)) + first
+    own = jnp.where(blocks[0, 0] == blocks[0, 1], own, -1)
+    other = residue_of(lax.broadcasted_iota(jnp.int32, (1, width), 1))
+    kept = jnp.where(own == other, 0.0, weights[0].astype(jnp.float32)).astype(jnp.bfloat16)
+    lead_table = table(states[:, :128], first, rows).astype(jnp.bfloat16)
+    lead[0] = lax.dot_general(
+        tail_table[...], kept, (((1,), (1,)), ((), ())), preferred_element_type=jnp.float32
+    )
+    tail[...] += jnp.dot(lead_table, kept, preferred_element_type=jnp.float32)
+
+
+def tile_fields(tile_blocks, states, couplings):
+    rows = states.shape[0]
+    return pl.pallas_call(
+        field_kernel,
+        grid=(WIDTH // ROW_TILE,),
+        out_shape=[
+            jax.ShapeDtypeStruct((WIDTH // ROW_TILE, rows, ROW_TILE), jnp.float32),
+            jax.ShapeDtypeStruct((rows, WIDTH), jnp.float32),
+        ],
+        in_specs=[
+            pl.BlockSpec(memory_space=pltpu.SMEM),
+            pl.BlockSpec((rows, 256), lambda i: (0, 0)),
+            pl.BlockSpec((1, ROW_TILE, WIDTH), lambda i: (0, i, 0)),
+        ],
+        out_specs=[
+            pl.BlockSpec((1, rows, ROW_TILE), lambda i: (i, 0, 0)),
+            pl.BlockSpec((rows, WIDTH), lambda i: (0, 0)),
+        ],
+        scratch_shapes=[pltpu.VMEM((rows, WIDTH), jnp.bfloat16)],
+        compiler_params=pltpu.CompilerParams(vmem_limit_bytes=40 << 20),
+    )(tile_blocks, states, couplings)
+
+
+def gradient_kernel(blocks, states, lead_probs, tail_probs, grad, left):
+    step = pl.program_id(0)
+    rows, share = lead_probs.shape
+    columns = tail_probs.shape[1]
+    first = lax.axis_index("seq") * (share // Q)
+
+    @pl.when(step == 0)
+    def _():
+        row = lax.broadcasted_iota(jnp.int32, (share, 128), 0)
+        lane = lax.broadcasted_iota(jnp.int32, (share, 128), 1)
+        place = (lane == residue_of(row) + first).astype(jnp.float32).astype(jnp.bfloat16)
+        spread = lax.dot_general(
+            place, states[:, :128], (((1,), (1,)), ((), ())), preferred_element_type=jnp.float32
+        )
+        row = lax.broadcasted_iota(jnp.int32, (share, 1), 0)
+        code = (row - residue_of(row) * Q).astype(jnp.float32)
+        lead_table = jnp.where(spread == code, 1.0, 0.0)
+        lead_gap = lead_probs[...].astype(jnp.float32).T - lead_table
+        left[:, :rows] = lead_gap.astype(jnp.bfloat16)
+        left[:, rows:] = lead_table.astype(jnp.bfloat16)
+
+    lanes = 128
+    start = step * columns
+    residue = residue_of(lax.broadcasted_iota(jnp.int32, (lanes, columns), 1) + start)
+    place = lax.broadcasted_iota(jnp.int32, (lanes, columns), 0) == residue
+    spread = jnp.dot(
+        states[:, 128:],
+        place.astype(jnp.float32).astype(jnp.bfloat16),
+        preferred_element_type=jnp.float32,
+    )
+    column = lax.broadcasted_iota(jnp.int32, (1, columns), 1) + start
+    other = residue_of(column)
+    code = (column - other * Q).astype(jnp.float32)
+    tail_table = jnp.where(spread == code, 1.0, 0.0)
+    tail_gap = (tail_probs[...].astype(jnp.float32) - tail_table).astype(jnp.bfloat16)
+    total = jnp.dot(
+        left[:, :rows], tail_table.astype(jnp.bfloat16), preferred_element_type=jnp.float32
+    )
+    total = total + jnp.dot(left[:, rows:], tail_gap, preferred_element_type=jnp.float32)
+    own = residue_of(lax.broadcasted_iota(jnp.int32, (share, 1), 0)) + first
+    own = jnp.where(blocks[0, 0] == blocks[0, 1], own, -1)
+    grad[...] = jnp.where(own == other, 0.0, total * (Q / math.sqrt(rows)))
+
+
+def gradient(tile_blocks, states, lead_probs, tail_probs):
+    rows, share = lead_probs.shape
+    return pl.pallas_call(
+        gradient_kernel,
+        grid=(pl.cdiv(WIDTH, COLUMN_TILE),),
+        out_shape=jax.ShapeDtypeStruct((share, WIDTH), jnp.float32),
+        in_specs=[
+            pl.BlockSpec(memory_space=pltpu.SMEM),
+            pl.BlockSpec((rows, 256), lambda i: (0, 0)),
+            pl.BlockSpec((rows, share), lambda i: (0, 0)),
+            pl.BlockSpec((rows, COLUMN_TILE), lambda i: (0, i)),
+        ],
+        out_specs=pl.BlockSpec((share, COLUMN_TILE), lambda i: (0, i)),
+        scratch_shapes=[pltpu.VMEM((share, 2 * rows), jnp.bfloat16)],
+        compiler_params=pltpu.CompilerParams(vmem_limit_bytes=40 << 20),
+    )(tile_blocks, states, lead_probs, tail_probs)
 
 
 def send(src, dst, send_sem, recv_sem, **device):
@@ -65,14 +183,32 @@
 
 
 def reduce_kernel(
-    groups, blocks, lead, tail, out, halves, mine, stage, mate_in, onward, arrived, sems
+    groups,
+    seqs,
+    blocks,
+    lead,
+    tail,
+    states,
+    out,
+    all_states,
+    halves,
+    mine,
+    stage,
+    mate_in,
+    onward,
+    arrived,
+    sems,
+    state_sems,
 ):
     tile = lax.axis_index("tile")
     group, core = tile // 2, tile % 2
     mate = group * 2 + 1 - core
     lead_block, tail_block = blocks[0, 0], blocks[0, 1]
+    seq = lax.axis_index("seq")
     for h in range(2):
-        halves[0, h] = lead[:, h * HALF : (h + 1) * HALF]
+        for j in range(lead.shape[0] // 2):
+            place = slice(j * ROW_TILE, (j + 1) * ROW_TILE)
+            halves[0, h, :, place] = lead[h * (lead.shape[0] // 2) + j]
         halves[1, h] = tail[:, h * HALF : (h + 1) * HALF]
 
     def part(g, h):
@@ -80,7 +216,12 @@
         in_tail = (tail_block == g).astype(jnp.float32)
         return (halves[0, h] * in_lead + halves[1, h] * in_tail).astype(jnp.bfloat16)
 
-    greet(groups, 0)
+    greet(groups, seqs)
+
+    def states_to(k):
+        other = (seq + k) % seqs
+        place = all_states.at[seq]
+        return send(states, place, state_sems.at[0, k], state_sems.at[1, k], seq=other)
 
     def to_mate(k):
         return send(stage.at[k], mate_in.at[k], sems.at[0, k], sems.at[1, k], tile=mate)
@@ -96,6 +237,13 @@
         return carry
 
     lax.fori_loop(0, groups, first, 0)
+
+    def start_states(k, carry):
+        states_to(k).start()
+        return carry
+
+    lax.fori_loop(1, seqs, start_states, 0)
+    all_states[seq] = states[...]
 
     def second(k, carry):
         mine[...] = part((group + k) % groups, core).astype(jnp.float32)
@@ -120,6 +268,12 @@
         return carry
 
     lax.fori_loop(0, groups, fourth, 0)
+
+    def finish_states(k, carry):
+        states_to(k).wait()
+        return carry
+
+    lax.fori_loop(1, seqs, finish_states, 0)
     out[...] = mine[...]
 
 
@@ -156,15 +310,18 @@
             lead_out.at[c, other], place, over.at[2, c, k], over.at[3, c, k], seq=other
         )
 
-    for c in range(CHUNKS):
+    def begin(c):
         every[c][group, core] = probs[c * rows : (c + 1) * rows]
 
-        def start_far(k, carry, c=c):
+        def start_far(k, carry):
             to_group(c, k).start()
             return carry
 
         lax.fori_loop(1, groups, start_far, 0)
         to_mate(c, 0).start()
+
+    begin(0)
+    begin(1)
 
     for c in range(CHUNKS):
 
@@ -174,6 +331,8 @@
             return carry
 
         lax.fori_loop(1, groups, relay, 0)
+        if c + 2 < CHUNKS:
+            begin(c + 2)
 
         def gathered(k, carry, c=c):
             to_mate(c, k).wait_recv()
@@ -217,15 +376,18 @@
         lax.fori_loop(0, groups, sent_pair, 0)
 
 
-def reduce_fields(tile_blocks, lead, tail, groups):
-    rows = lead.shape[0]
+def reduce_fields(tile_blocks, lead, tail, states, groups, seqs):
+    rows = tail.shape[0]
     slots = pltpu.VMEM((groups, rows, HALF), jnp.bfloat16)
     vmem = pl.BlockSpec(memory_space=pltpu.VMEM)
     return pl.pallas_call(
-        functools.partial(reduce_kernel, groups),
-        out_shape=jax.ShapeDtypeStruct((rows, HALF), jnp.float32),
-        in_specs=[pl.BlockSpec(memory_space=pltpu.SMEM), vmem, vmem],
-        out_specs=vmem,
+        functools.partial(reduce_kernel, groups, seqs),
+        out_shape=[
+            jax.ShapeDtypeStruct((rows, HALF), jnp.float32),
+            jax.ShapeDtypeStruct((seqs,) + states.shape, jnp.bfloat16),
+        ],
+        in_specs=[pl.BlockSpec(memory_space=pltpu.SMEM), vmem, vmem, vmem],
+        out_specs=[vmem, vmem],
         scratch_shapes=[
             pltpu.VMEM((2, 2, rows, HALF), jnp.float32),
             pltpu.VMEM((rows, HALF), jnp.float32),
@@ -234,11 +396,12 @@
             slots,
             slots,
             pltpu.SemaphoreType.DMA((4, groups)),
+            pltpu.SemaphoreType.DMA((2, seqs)),
         ],
         compiler_params=pltpu.CompilerParams(
             collective_id=0, has_side_effects=True, vmem_limit_bytes=48 << 20
         ),
-    )(tile_blocks, lead, tail)
+    )(tile_blocks, lead, tail, states)
 
 
 def exchange(tile_blocks, probs, groups, seqs):
@@ -270,47 +433,26 @@
 def body(states, tile_blocks, couplings, fields):
     groups = lax.axis_size("tile") // 2
     seqs = lax.axis_size("seq")
-    seq = lax.axis_index("seq")
     row_total = states.shape[0] * seqs
     share = WIDTH // seqs
-    lead_block = tile_blocks[0, 0]
-    tail_block = tile_blocks[0, 1]
-    apart = lead_block != tail_block
-    residue = jnp.arange(WIDTH, dtype=jnp.int32) // Q
-    keep_mask = jnp.logical_or(apart, residue[:, None] != residue[None, :])
-    masked = jnp.where(keep_mask, couplings[0], jnp.zeros((), jnp.bfloat16))
-    lead_states = lax.dynamic_slice_in_dim(states, lead_block * LB, LB, 1)
-    tail_states = lax.dynamic_slice_in_dim(states, tail_block * LB, LB, 1)
-    both_states = lax.all_gather(
-        jnp.concatenate([lead_states, tail_states], axis=1), "seq", axis=0, tiled=True
-    )
-    lead = lax.dot_general(
-        state_table(tail_states),
-        masked,
-        (((1,), (1,)), ((), ())),
-        preferred_element_type=jnp.float32,
-    )
-    tail = jnp.dot(state_table(lead_states), masked, preferred_element_type=jnp.float32)
-    logits = reduce_fields(tile_blocks, lead, tail, groups)
+    picked = [
+        jnp.pad(
+            lax.dynamic_slice_in_dim(states, tile_blocks[0, side] * LB, LB, 1),
+            ((0, 0), (0, 128 - LB)),
+        )
+        for side in range(2)
+    ]
+    own_states = jnp.concatenate(picked, axis=1).astype(jnp.bfloat16)
+    lead, tail = tile_fields(tile_blocks, own_states, couplings)
+    logits, all_states = reduce_fields(tile_blocks, lead, tail, own_states, groups, seqs)
     probs = normalize(logits + fields[None, :])
     tail_probs, lead_probs = exchange(tile_blocks, probs, groups, seqs)
-    tail_probs = tail_probs.reshape(row_total, WIDTH)
-    lead_probs = lead_probs.reshape(row_total, share)
-    share_states = lax.dynamic_slice_in_dim(both_states, seq * (LB // seqs), LB // seqs, 1)
-    lead_table = state_table(share_states)
-    tail_table = state_table(both_states[:, LB:])
-    lead_gap = lead_probs - lead_table
-    tail_gap = tail_probs - tail_table
-    grad = lax.dot_general(
-        lead_gap, tail_table, (((0,), (0,)), ((), ())), preferred_element_type=jnp.float32
-    )
-    grad = grad + lax.dot_general(
-        lead_table, tail_gap, (((0,), (0,)), ((), ())), preferred_element_type=jnp.float32
-    )
-    grad_scale = Q / math.sqrt(row_total)
-    own_residue = seq * (LB // seqs) + jnp.arange(share, dtype=jnp.int32) // Q
-    own_mask = jnp.logical_or(apart, own_residue[:, None] != residue[None, :])
-    grad = jnp.where(own_mask, grad * grad_scale, jnp.zeros((), jnp.float32))
+    grad = gradient(
+        tile_blocks,
+        all_states.reshape(row_total, 256),
+        lead_probs.reshape(row_total, share),
+        tail_probs.reshape(row_total, WIDTH),
+    )
     return (probs, grad[None])
 
 

time: 148 us -> 101 us (0.68)
  matrix products: 22.3 us -> 0 us
  local copies, waits for them, and re-layouts: 26.1 us -> 6.93 us
  Pallas kernels: 73.7 us -> 87.2 us
  blocking collectives: 11.8 us -> 0 us
  other arithmetic: 9.22 us -> 2.76 us
    dot_general x4 -> x0, matrix products: 22.3 us -> none  [the longest x1 6 us: body(): jnp.dot(state_table(lead_states), masked, preferred_element_type=jnp.floa...]
    eq x14 -> x0, local copies, waits for them, and re-layouts: 18.4 us -> none  [state_table(): matches = block_states[:, :, None] == state_codes[None, None, :]]
    pallas_call x1 -> x3, Pallas kernels: 28.6 us -> 41.4 us  [the longest x1 28.7 us: reduce_fields(): pl.pallas_call(functools.partial(reduce_kernel, groups, seqs), out_shape=...]
    all_gather x1 -> x0, blocking collectives: 11.8 us -> none  [body(): lax.all_gather(jnp.concatenate([lead_states, tail_states], axis=1), 'seq'...]
    sub x2 -> x0, other arithmetic: 5.23 us -> none  [the longest x1 4.23 us: body(): tail_gap = tail_probs - tail_table]
    unnamed x11 -> x9, local copies, waits for them, and re-layouts: 1.51 us -> 4.87 us
    slice x3 -> x1, local copies, waits for them, and re-layouts: 3.91 us -> 1.31 us  [body(): tile_blocks[0, side] * LB]
    eq x4 -> x0, other arithmetic: 2.21 us -> none  [state_table(): matches = block_states[:, :, None] == state_codes[None, None, :]]
where the time goes in v2:
time: 101 us; the launch traced here: 99 us
  Pallas kernels  87.2 us (86%)
  local copies, waits for them, and re-layouts  6.93 us (7%)
  other arithmetic  2.76 us (3%)
  between operations  2.08 us (2%)
    pallas_call x1, Pallas kernels, exchange(): pl.pallas_call(functools.partial(exchange_kernel, groups, seqs), out_shap...  45.8 us
    pallas_call x1, Pallas kernels, reduce_fields(): pl.pallas_call(functools.partial(reduce_kernel, groups, seqs), out_shape=...  28.7 us
    pallas_call x1, Pallas kernels, tile_fields(): pl.pallas_call(field_kernel, grid=(WIDTH // ROW_TILE,), out_shape=[jax.Sh...  6.65 us
    pallas_call x1, Pallas kernels, gradient(): pl.pallas_call(gradient_kernel, grid=(pl.cdiv(WIDTH, COLUMN_TILE),), out_...  6.03 us
    unnamed x9, local copies, waits for them, and re-layouts  4.87 us

profile of v2, /device:TPU:28, one launch (start us, length us, event | category | flops | bytes accessed | tf_op | source)
XLA Modules:
  0.0 99.0 jit_solution(5313442931388277960)
XLA Ops:
  0.6 1.3 %fusion.7 = (s32[1,1]{1,0:T(1,128)}, s32[1,1]{1,0:T(1,128)}) fusion(s32[1,2]{1,0:T(1,128)} %blocks.7), kind=kLoop, calls=%fused_computation.14 | loop fusion | bytes 16 | tf_op jit(solution)/shard_map/slice | solution.py:440
  3.3 1.1 %dynamic-slice_convert_fusion.1 = (bf16[128,96]{1,0:T(8,128)(2,1)S(1)}, bf16[128,96]{1,0:T(8,128)(2,1)S(1)}) fusion(s32[128,384]{1,0:T(8,128)} %param.4, s32[]{:T(128)S(6)} %select_n.6, s32[]{:T(128)S(6)} %select_n.7), kind=kLoop, calls=%fused_computation.13 | loop fusion | flops 24576 | bytes 147464 | tf_op jit(solution)/shard_map/convert.4
  4.4 0.0 copy-start
  4.4 3.3 %copy-done = bf16[1,2016,2016]{2,1,0:T(8,128)(2,1)S(1)} copy-done((bf16[1,2016,2016]{2,1,0:T(8,128)(2,1)S(1)}, bf16[1,2016,2016]{2,1,0:T(8,128)(2,1)}, u32[]{:S(2)}) %copy-start) | copy-done | bytes 8128536
  7.7 0.0 copy-start.1
  7.7 0.7 copy-done.1
  8.4 0.0 copy-start.2
  8.4 0.0 copy-start.3
  8.4 6.7 %shard_map.59 = (f32[6,128,336]{2,1,0:T(8,128)S(1)}, f32[128,2016]{1,0:T(8,128)S(1)}) custom-call(s32[1,2]{1,0:T(1,128)S(1)} %copy-done.1, bf16[128,256]{1,0:T(8,128)(2,1)S(1)} %fusion.6.states, bf16[1,2016,2016]{2,1,0:T(8,128)(2,1)S(1)} %copy-done), custom_call_target="tpu_custom_call" | custom-call | tf_op jit(solution)/shard_map/pallas_call | solution.py:68
  15.0 0.0 copy-done.2
  15.0 28.7 %shard_map.60 = (f32[128,1008]{1,0:T(8,128)S(1)}, bf16[4,128,256]{2,1,0:T(8,128)(2,1)S(1)}) custom-call(s32[1,2]{1,0:T(1,128)S(1)} %copy-done.2, f32[6,128,336]{2,1,0:T(8,128)S(1)} %get-tuple-element.8.lead, f32[128,2016]{1,0:T(8,128)S(1)} %get-tuple-element.9.tail, bf16[128,256]{1,0:T(8,128)(2,1)S(1)} %fusion.6.states), custom_call_target="tpu_custom_call" | custom-call | tf_op jit(solution)/shard_map/pallas_call | solution.py:383
  43.8 0.0 copy-done.3
  43.9 0.2 copy.7
  44.1 0.1 reduce_max.9
  44.2 1.3 %fusion = f32[128,48,21]{0,2,1:T(8,128)S(1)} fusion(f32[128,48,21]{0,2,1:T(8,128)S(1)} %reshape.26, f32[128,48]{0,1:T(8,128)S(1)} %reduce_max.9), kind=kOutput, calls=%fused_computation | output fusion | flops 135188 | bytes 1056768 | tf_op jit(solution)/shard_map/div | solution.py:41
  45.6 0.2 copy.9
  45.9 0.2 copy.8
  46.1 0.2 divide_convert_fusion.probs
  46.3 0.9 copy.10
  47.2 45.8 %shard_map.61 = (bf16[4,128,2016]{2,1,0:T(8,128)(2,1)S(1)}, bf16[4,128,504]{2,1,0:T(8,128)(2,1)S(1)}) custom-call(s32[1,2]{1,0:T(1,128)S(1)} %copy-done.2, bf16[128,1008]{1,0:T(8,128)(2,1)S(1)} %divide_convert_fusion.probs), custom_call_target="tpu_custom_call" | custom-call | tf_op jit(solution)/shard_map/pallas_call | solution.py:411
  92.9 6.0 %shard_map.62 = f32[504,2016]{1,0:T(8,128)} custom-call(s32[1,2]{1,0:T(1,128)S(1)} %copy-done.2, bf16[512,256]{1,0:T(8,128)(2,1)S(1)} %bitcast.14, bf16[512,504]{1,0:T(8,128)(2,1)S(1)} %bitcast.13, bf16[512,2016]{1,0:T(8,128)(2,1)S(1)} %bitcast.12), custom_call_target="tpu_custom_call" | custom-call | tf_op jit(solution)/shard_map/pallas_call | solution.py:135
  (6 shorter events, 0.2 us)
Async XLA Ops:
  4.4 3.3 %copy-start = (bf16[1,2016,2016]{2,1,0:T(8,128)(2,1)S(1)}, bf16[1,2016,2016]{2,1,0:T(8,128)(2,1)}, u32[]{:S(2)}) copy-start(bf16[1,2016,2016]{2,1,0:T(8,128)(2,1)} %weights.1) | copy-start | bytes 24385540
  7.7 0.7 copy-start.1
  8.4 6.7 %copy-start.2 = (s32[1,2]{1,0:T(1,128)S(1)}, s32[1,2]{1,0:T(1,128)}, u32[]{:S(2)}) copy-start(s32[1,2]{1,0:T(1,128)} %blocks.7) | copy-start | bytes 28
  8.4 35.4 %copy-start.3 = (f32[1008]{0:T(1024)S(1)}, f32[1008]{0:T(1024)}, u32[]{:S(2)}) copy-start(f32[1008]{0:T(1024)} %param.7) | copy-start | bytes 12100

commit v3 on v2

v3 whole, which is shorter than its diff:
```python
import functools
import math

import jax
import jax.numpy as jnp
from jax import lax
from jax.experimental import pallas as pl
from jax.experimental.pallas import tpu as pltpu
from jax.sharding import PartitionSpec as P

Q = 21
LB = 96
WIDTH = LB * Q
HALF = WIDTH // 2
CHUNKS = 4
ROW_TILE = WIDTH // 6
COLUMN_TILE = 512


def residue_of(index):
    return (index * 3121) >> 16


def table(states, first, columns):
    lanes = states.shape[1]
    residue = residue_of(lax.broadcasted_iota(jnp.int32, (lanes, columns), 1)) + first
    place = lax.broadcasted_iota(jnp.int32, (lanes, columns), 0) == residue
    spread = jnp.dot(
        states, place.astype(jnp.float32).astype(jnp.bfloat16), preferred_element_type=jnp.float32
    )
    column = lax.broadcasted_iota(jnp.int32, (1, columns), 1)
    code = (column - residue_of(column) * Q).astype(jnp.float32)
    return jnp.where(spread == code, 1.0, 0.0)


def normalize(logits):
    lanes = logits.shape[1]
    lane = lax.broadcasted_iota(jnp.int32, (1, lanes), 1)
    place = lane - residue_of(lane) * Q
    shifts = (1, 2, 4, 8, 16)
    top = logits
    for shift in shifts:
        top = jnp.where(place >= shift, jnp.maximum(top, pltpu.roll(top, shift, 1)), top)
    for shift in shifts:
        back = pltpu.roll(top, lanes - shift, 1)
        top = jnp.where(place + shift < Q, jnp.maximum(top, back), top)
    exponent = jnp.exp(logits - top)
    total = exponent
    for shift in shifts:
        total = total + jnp.where(place >= shift, pltpu.roll(total, shift, 1), 0.0)
    total = jnp.where(place == Q - 1, total, 0.0)
    for shift in shifts:
        back = pltpu.roll(total, lanes - shift, 1)
        total = jnp.where(place + shift < Q, jnp.maximum(total, back), total)
    return exponent / total


def field_kernel(blocks, codes, weights, lead, tail, tail_table, states):
    step = pl.program_id(0)
    rows, width = weights.shape[1], weights.shape[2]
    first = step * (rows // Q)

    @pl.when(step == 0)
    def _():
        states[...] = codes[...].astype(jnp.float32).astype(jnp.bfloat16)
        tail_table[...] = table(states[...], blocks[0, 1] * LB, width).astype(jnp.bfloat16)
        tail[...] = jnp.zeros_like(tail)

    own = residue_of(lax.broadcasted_iota(jnp.int32, (rows, 1), 0)) + first
    own = jnp.where(blocks[0, 0] == blocks[0, 1], own, -1)
    other = residue_of(lax.broadcasted_iota(jnp.int32, (1, width), 1))
    kept = jnp.where(own == other, 0.0, weights[0].astype(jnp.float32)).astype(jnp.bfloat16)
    lead_table = table(states[...], blocks[0, 0] * LB + first, rows).astype(jnp.bfloat16)
    lead[0] = lax.dot_general(
        tail_table[...], kept, (((1,), (1,)), ((), ())), preferred_element_type=jnp.float32
    )
    tail[...] += jnp.dot(lead_table, kept, preferred_element_type=jnp.float32)


def tile_fields(tile_blocks, states, couplings):
    rows = states.shape[0]
    return pl.pallas_call(
        field_kernel,
        grid=(WIDTH // ROW_TILE,),
        out_shape=[
            jax.ShapeDtypeStruct((WIDTH // ROW_TILE, rows, ROW_TILE), jnp.float32),
            jax.ShapeDtypeStruct((rows, WIDTH), jnp.float32),
        ],
        in_specs=[
            pl.BlockSpec(memory_space=pltpu.SMEM),
            pl.BlockSpec(states.shape, lambda i: (0, 0)),
            pl.BlockSpec((1, ROW_TILE, WIDTH), lambda i: (0, i, 0)),
        ],
        out_specs=[
            pl.BlockSpec((1, rows, ROW_TILE), lambda i: (i, 0, 0)),
            pl.BlockSpec((rows, WIDTH), lambda i: (0, 0)),
        ],
        scratch_shapes=[
            pltpu.VMEM((rows, WIDTH), jnp.bfloat16),
            pltpu.VMEM(states.shape, jnp.bfloat16),
        ],
        compiler_params=pltpu.CompilerParams(vmem_limit_bytes=60 << 20),
    )(tile_blocks, states, couplings)


def gradient_kernel(blocks, states, lead_probs, tail_probs, grad, left):
    step = pl.program_id(0)
    rows, share = lead_probs.shape
    columns = tail_probs.shape[1]
    first = lax.axis_index("seq") * (share // Q)
    lanes = states.shape[1]

    @pl.when(step == 0)
    def _():
        row = lax.broadcasted_iota(jnp.int32, (share, lanes), 0)
        lane = lax.broadcasted_iota(jnp.int32, (share, lanes), 1)
        here = residue_of(row) + first + blocks[0, 0] * LB
        place = (lane == here).astype(jnp.float32).astype(jnp.bfloat16)
        spread = lax.dot_general(
            place, states[...], (((1,), (1,)), ((), ())), preferred_element_type=jnp.float32
        )
        row = lax.broadcasted_iota(jnp.int32, (share, 1), 0)
        code = (row - residue_of(row) * Q).astype(jnp.float32)
        lead_table = jnp.where(spread == code, 1.0, 0.0)
        lead_gap = lead_probs[...].astype(jnp.float32).T - lead_table
        left[:, :rows] = lead_gap.astype(jnp.bfloat16)
        left[:, rows:] = lead_table.astype(jnp.bfloat16)

    start = step * columns
    residue = residue_of(lax.broadcasted_iota(jnp.int32, (lanes, columns), 1) + start)
    here = residue + blocks[0, 1] * LB
    place = lax.broadcasted_iota(jnp.int32, (lanes, columns), 0) == here
    spread = jnp.dot(
        states[...],
        place.astype(jnp.float32).astype(jnp.bfloat16),
        preferred_element_type=jnp.float32,
    )
    column = lax.broadcasted_iota(jnp.int32, (1, columns), 1) + start
    other = residue_of(column)
    code = (column - other * Q).astype(jnp.float32)
    tail_table = jnp.where(spread == code, 1.0, 0.0)
    tail_gap = (tail_probs[...].astype(jnp.float32) - tail_table).astype(jnp.bfloat16)
    total = jnp.dot(
        left[:, :rows], tail_table.astype(jnp.bfloat16), preferred_element_type=jnp.float32
    )
    total = total + jnp.dot(left[:, rows:], tail_gap, preferred_element_type=jnp.float32)
    own = residue_of(lax.broadcasted_iota(jnp.int32, (share, 1), 0)) + first
    own = jnp.where(blocks[0, 0] == blocks[0, 1], own, -1)
    grad[...] = jnp.where(own == other, 0.0, total * (Q / math.sqrt(rows)))


def gradient(tile_blocks, states, lead_probs, tail_probs):
    rows, share = lead_probs.shape
    return pl.pallas_call(
        gradient_kernel,
        grid=(pl.cdiv(WIDTH, COLUMN_TILE),),
        out_shape=jax.ShapeDtypeStruct((share, WIDTH), jnp.float32),
        in_specs=[
            pl.BlockSpec(memory_space=pltpu.SMEM),
            pl.BlockSpec(states.shape, lambda i: (0, 0)),
            pl.BlockSpec((rows, share), lambda i: (0, 0)),
            pl.BlockSpec((rows, COLUMN_TILE), lambda i: (0, i)),
        ],
        out_specs=pl.BlockSpec((share, COLUMN_TILE), lambda i: (0, i)),
        scratch_shapes=[pltpu.VMEM((share, 2 * rows), jnp.bfloat16)],
        compiler_params=pltpu.CompilerParams(vmem_limit_bytes=40 << 20),
    )(tile_blocks, states, lead_probs, tail_probs)


def send(src, dst, send_sem, recv_sem, **device):
    return pltpu.make_async_remote_copy(
        src_ref=src,
        dst_ref=dst,
        send_sem=send_sem,
        recv_sem=recv_sem,
        device_id=device,
        device_id_type=pl.DeviceIdType.MESH,
    )


def greet(groups, seqs):
    tile = lax.axis_index("tile")
    group, core = tile // 2, tile % 2
    seq = lax.axis_index("seq")
    barrier = pltpu.get_barrier_semaphore()
    mesh_id = pl.DeviceIdType.MESH
    pl.semaphore_signal(
        barrier, inc=1, device_id={"tile": group * 2 + 1 - core}, device_id_type=mesh_id
    )
    for k in range(1, groups):
        pl.semaphore_signal(
            barrier,
            inc=1,
            device_id={"tile": ((group + k) % groups) * 2 + core},
            device_id_type=mesh_id,
        )
    for k in range(1, seqs):
        pl.semaphore_signal(
            barrier, inc=1, device_id={"seq": (seq + k) % seqs}, device_id_type=mesh_id
        )
    pl.semaphore_wait(barrier, groups + max(seqs - 1, 0))


def exchange_kernel(
    groups, seqs, blocks, lead, tail, codes, fields, probs, tails, leads, states, *scratch
):
    every = scratch[:CHUNKS]
    tail_out = scratch[CHUNKS : 2 * CHUNKS]
    (lead_out, halves, logits, stage, mate_in, onward, arrived) = scratch[2 * CHUNKS : -6]
    (halved, summed, near, pair, over, shared) = scratch[-6:]
    tile = lax.axis_index("tile")
    group, core = tile // 2, tile % 2
    seq = lax.axis_index("seq")
    mate = group * 2 + 1 - core
    lead_block, tail_block = blocks[0, 0], blocks[0, 1]
    rows = probs.shape[0] // CHUNKS
    share = WIDTH // seqs
    for h in range(2):
        for j in range(lead.shape[0] // 2):
            place = slice(j * ROW_TILE, (j + 1) * ROW_TILE)
            halves[0, h, :, place] = lead[h * (lead.shape[0] // 2) + j]
        halves[1, h] = tail[:, h * HALF : (h + 1) * HALF]
    states[seq] = codes[...].astype(jnp.float32).astype(jnp.bfloat16)
    logits[...] = jnp.zeros_like(logits)
    greet(groups, seqs)

    def part(c, g, h):
        in_lead = (lead_block == g).astype(jnp.float32)
        in_tail = (tail_block == g).astype(jnp.float32)
        here = slice(c * rows, (c + 1) * rows)
        value = halves[0, h, here] * in_lead + halves[1, h, here] * in_tail
        return value.astype(jnp.bfloat16)

    def half_to_mate(c, k):
        return send(
            stage.at[c, k], mate_in.at[c, k], halved.at[0, c, k], halved.at[1, c, k], tile=mate
        )

    def sum_to_owner(c, k):
        owner = ((group + k) % groups) * 2 + core
        return send(
            onward.at[c, k], arrived.at[c, k], summed.at[0, c, k], summed.at[1, c, k], tile=owner
        )

    def to_group(c, k):
        other = ((group + k) % groups) * 2 + core
        mine = every[c].at[group, core]
        return send(mine, mine, near.at[0, c, k], near.at[1, c, k], tile=other)

    def to_mate(c, k):
        block = every[c].at[(group + groups - k) % groups, core]
        return send(block, block, pair.at[0, c, k], pair.at[1, c, k], tile=mate)

    def tail_to(c, k):
        place = tails.at[seq, pl.ds(c * rows, rows)]
        return send(tail_out[c], place, over.at[0, c, k], over.at[1, c, k], seq=(seq + k) % seqs)

    def lead_to(c, k):
        other = (seq + k) % seqs
        place = leads.at[seq, pl.ds(c * rows, rows)]
        return send(
            lead_out.at[c, other], place, over.at[2, c, k], over.at[3, c, k], seq=other
        )

    def states_to(k):
        own = states.at[seq]
        return send(own, own, shared.at[0, k], shared.at[1, k], seq=(seq + k) % seqs)

    def each(low, high, act):
        def step(k, carry):
            act(k)
            return carry

        lax.fori_loop(low, high, step, 0)

    def halve(c):
        def act(k):
            k = (k + 1) % groups
            stage[c, k] = part(c, (group + k) % groups, 1 - core)
            half_to_mate(c, k).start()

        each(0, groups, act)

    def reduce_start(c):
        def act(k):
            own = part(c, (group + k) % groups, core).astype(jnp.float32)
            half_to_mate(c, k).wait_recv()
            onward[c, k] = (own + mate_in[c, k].astype(jnp.float32)).astype(jnp.bfloat16)
            sum_to_owner(c, k).start()

        each(1, groups, act)

    def reduce_end(c):
        half_to_mate(c, 0).wait_recv()
        own = part(c, group, core).astype(jnp.float32) + mate_in[c, 0].astype(jnp.float32)
        logits[:, :HALF] = own + fields[...]

        def act(k):
            sum_to_owner(c, k).wait_recv()
            logits[:, :HALF] += arrived[c, k].astype(jnp.float32)

        each(1, groups, act)
        result = normalize(logits[...])[:, :HALF].astype(jnp.bfloat16)
        every[c][group, core] = result
        each(1, groups, lambda k: to_group(c, k).start())
        to_mate(c, 0).start()
        probs[c * rows : (c + 1) * rows] = result

    def relay(c):
        def act(k):
            to_group(c, k).wait_recv()
            to_mate(c, k).start()

        each(1, groups, act)
        each(0, groups, lambda k: to_mate(c, k).wait_recv())
        for h in range(2):
            tail_out[c][:, h * HALF : (h + 1) * HALF] = every[c][tail_block, h]
            block_half = every[c][lead_block, h]
            for j in range(seqs // 2):
                lead_out[c, h * (seqs // 2) + j] = block_half[:, j * share : (j + 1) * share]

        def start(k):
            tail_to(c, k).start()
            lead_to(c, k).start()

        each(1, seqs, start)
        tails[seq, c * rows : (c + 1) * rows] = tail_out[c][...]
        leads[seq, c * rows : (c + 1) * rows] = lead_out[c, seq]

    def finish(c):
        def ends(k):
            tail_to(c, k).wait()
            lead_to(c, k).wait()

        each(1, seqs, ends)

        def sent(k):
            to_group(c, k).wait_send()
            sum_to_owner(c, k).wait_send()

        each(1, groups, sent)

        def passed(k):
            to_mate(c, k).wait_send()
            half_to_mate(c, k).wait_send()

        each(0, groups, passed)

    halve(0)
    halve(1)
    reduce_start(0)
    each(1, seqs, lambda k: states_to(k).start())
    reduce_start(1)
    for c in range(2, CHUNKS):
        halve(c)
    for c in range(CHUNKS + 1):
        if c < CHUNKS:
            reduce_end(c)
        if c + 2 < CHUNKS:
            reduce_start(c + 2)
        if c > 0:
            relay(c - 1)
    for c in range(CHUNKS):
        finish(c)
    each(1, seqs, lambda k: states_to(k).wait())


def exchange(tile_blocks, lead, tail, states, fields, groups, seqs):
    rows = tail.shape[0]
    part = rows // CHUNKS
    vmem = pl.BlockSpec(memory_space=pltpu.VMEM)
    slots = pltpu.VMEM((CHUNKS, groups, part, HALF), jnp.bfloat16)
    pair_sems = pltpu.SemaphoreType.DMA((2, CHUNKS, groups))
    return pl.pallas_call(
        functools.partial(exchange_kernel, groups, seqs),
        out_shape=[
            jax.ShapeDtypeStruct((rows, HALF), jnp.bfloat16),
            jax.ShapeDtypeStruct((seqs, rows, WIDTH), jnp.bfloat16),
            jax.ShapeDtypeStruct((seqs, rows, WIDTH // seqs), jnp.bfloat16),
            jax.ShapeDtypeStruct((seqs,) + states.shape, jnp.bfloat16),
        ],
        in_specs=[pl.BlockSpec(memory_space=pltpu.SMEM)] + [vmem] * 4,
        out_specs=[vmem] * 4,
        scratch_shapes=[pltpu.VMEM((groups, 2, part, HALF), jnp.bfloat16)] * CHUNKS
        + [pltpu.VMEM((part, WIDTH), jnp.bfloat16)] * CHUNKS
        + [
            pltpu.VMEM((CHUNKS, seqs, part, WIDTH // seqs), jnp.bfloat16),
            pltpu.VMEM((2, 2, rows, HALF), jnp.float32),
            pltpu.VMEM((part, 1024), jnp.float32),
            slots,
            slots,
            slots,
            slots,
            pair_sems,
            pair_sems,
            pair_sems,
            pair_sems,
            pltpu.SemaphoreType.DMA((4, CHUNKS, seqs)),
            pltpu.SemaphoreType.DMA((2, seqs)),
        ],
        compiler_params=pltpu.CompilerParams(
            collective_id=0, has_side_effects=True, vmem_limit_bytes=60 << 20
        ),
    )(tile_blocks, lead, tail, states, fields)


def body(states, tile_blocks, couplings, fields):
    groups = lax.axis_size("tile") // 2
    seqs = lax.axis_size("seq")
    row_total = states.shape[0] * seqs
    share = WIDTH // seqs
    lead, tail = tile_fields(tile_blocks, states, couplings)
    probs, tail_probs, lead_probs, all_states = exchange(
        tile_blocks, lead, tail, states, fields[None, :], groups, seqs
    )
    grad = gradient(
        tile_blocks,
        all_states.reshape(row_total, states.shape[1]),
        lead_probs.reshape(row_total, share),
        tail_probs.reshape(row_total, WIDTH),
    )
    return (probs, grad[None])


def solution(mesh):
    in_specs = (P("seq", None), P("tile", None), P("tile", None, None), P("tile"))
    out_specs = (P("seq", "tile"), P("tile", "seq", None))
    return jax.shard_map(body, mesh=mesh, in_specs=in_specs, out_specs=out_specs, check_vma=False)
```

time: 101 us -> 93.2 us (0.923); the launches traced: 99 us -> 92.7 us
  other arithmetic: 2.76 us -> 0 us
  local copies, waits for them, and re-layouts: 6.93 us -> 5.45 us
  between operations: 2.08 us -> 0.65 us
    pallas_call x1 -> x0, Pallas kernels: 28.7 us -> none  [reduce_fields(): pl.pallas_call(functools.partial(reduce_kernel, groups, seqs), out_shape=...]
    pallas_call x1, Pallas kernels: 45.8 us -> 70.2 us  [exchange(): pl.pallas_call(functools.partial(exchange_kernel, groups, seqs), out_shap...]
    pallas_call x1, Pallas kernels: 6.65 us -> 9.6 us  [tile_fields(): pl.pallas_call(field_kernel, grid=(WIDTH // ROW_TILE,), out_shape=[jax.Sh...]
    div x1 -> x0, other arithmetic: 1.32 us -> none  [normalize(): result = exponent / jnp.sum(exponent, axis=2, keepdims=True)]
    slice x1 -> x0, local copies, waits for them, and re-layouts: 1.31 us -> none  [body(): tile_blocks[0, side] * LB]
    another operation x1 -> x0, other arithmetic: 1.09 us -> none
where the time goes in v3:
time: 93.2 us; the launch traced here: 92.7 us
  Pallas kernels  86.6 us (93%)
  local copies, waits for them, and re-layouts  5.45 us (6%)
    pallas_call x1, Pallas kernels, exchange(): pl.pallas_call(functools.partial(exchange_kernel, groups, seqs), out_shap...  70.2 us
    pallas_call x1, Pallas kernels, tile_fields(): pl.pallas_call(field_kernel, grid=(WIDTH // ROW_TILE,), out_shape=[jax.Sh...  9.6 us
    pallas_call x1, Pallas kernels, gradient(): pl.pallas_call(gradient_kernel, grid=(pl.cdiv(WIDTH, COLUMN_TILE),), out_...  6.8 us
    unnamed x9, local copies, waits for them, and re-layouts  5.45 us

profile of v3, /device:TPU:28, one launch (start us, length us, event | category | flops | bytes accessed | tf_op | source)
XLA Modules:
  0.0 92.7 jit_solution(13888389423993021110)
XLA Ops:
  0.6 0.0 copy-start.3
  0.6 9.6 %shard_map.59 = (f32[6,128,336]{2,1,0:T(8,128)}, f32[128,2016]{1,0:T(8,128)}) custom-call(s32[1,2]{1,0:T(1,128)} %blocks.5, s32[128,384]{1,0:T(8,128)} %codes.3, bf16[1,2016,2016]{2,1,0:T(8,128)(2,1)} %weights.1), custom_call_target="tpu_custom_call" | custom-call | tf_op jit(solution)/shard_map/pallas_call | solution.py:82
  10.2 70.2 %shard_map.60 = (bf16[128,1008]{1,0:T(8,128)(2,1)}, bf16[4,128,2016]{2,1,0:T(8,128)(2,1)}, bf16[4,128,504]{2,1,0:T(8,128)(2,1)}, bf16[4,128,384]{2,1,0:T(8,128)(2,1)}) custom-call(s32[1,2]{1,0:T(1,128)} %blocks.5, f32[6,128,336]{2,1,0:T(8,128)} %get-tuple-element.8.lead, f32[128,2016]{1,0:T(8,128)} %get-tuple-element.9.tail, s32[128,384]{1,0:T(8,128)} %codes.3, ...), custom_call_target="tpu_custom_call" | custom-call | tf_op jit(solution)/shard_map/pallas_call | solution.py:374
  80.5 1.8 %copy.6 = bf16[128,1008]{0,1:T(8,128)(2,1)} copy(bf16[128,1008]{1,0:T(8,128)(2,1)} %get-tuple-element.14) | data formatting | bytes 516096
  82.3 0.0 copy-done.3
  82.3 0.0 copy-start
  82.3 1.6 %copy-done = bf16[4,128,2016]{2,1,0:T(8,128)(2,1)S(1)} copy-done((bf16[4,128,2016]{2,1,0:T(8,128)(2,1)S(1)}, bf16[4,128,2016]{2,1,0:T(8,128)(2,1)}, u32[]{:S(2)}) %copy-start) | copy-done | bytes 2064408
  83.9 0.0 copy-start.1
  83.9 1.0 %copy-done.1 = bf16[4,128,504]{2,1,0:T(8,128)(2,1)S(1)} copy-done((bf16[4,128,504]{2,1,0:T(8,128)(2,1)S(1)}, bf16[4,128,504]{2,1,0:T(8,128)(2,1)}, u32[]{:S(2)}) %copy-start.1) | copy-done | bytes 516120
  84.9 0.0 copy-start.2
  84.9 1.0 %copy-done.2 = bf16[4,128,384]{2,1,0:T(8,128)(2,1)S(1)} copy-done((bf16[4,128,384]{2,1,0:T(8,128)(2,1)S(1)}, bf16[4,128,384]{2,1,0:T(8,128)(2,1)}, u32[]{:S(2)}) %copy-start.2) | copy-done | bytes 393240
  85.9 6.8 %shard_map.61 = f32[504,2016]{1,0:T(8,128)} custom-call(s32[1,2]{1,0:T(1,128)S(1)} %copy-done.3, bf16[512,384]{1,0:T(8,128)(2,1)S(1)} %bitcast.7, bf16[512,504]{1,0:T(8,128)(2,1)S(1)} %bitcast.6, bf16[512,2016]{1,0:T(8,128)(2,1)S(1)} %bitcast.5), custom_call_target="tpu_custom_call" | custom-call | tf_op jit(solution)/shard_map/pallas_call | solution.py:154
Async XLA Ops:
  0.6 81.7 %copy-start.3 = (s32[1,2]{1,0:T(1,128)S(1)}, s32[1,2]{1,0:T(1,128)}, u32[]{:S(2)}) copy-start(s32[1,2]{1,0:T(1,128)} %blocks.5) | copy-start | bytes 28
  82.3 1.6 %copy-start = (bf16[4,128,2016]{2,1,0:T(8,128)(2,1)S(1)}, bf16[4,128,2016]{2,1,0:T(8,128)(2,1)}, u32[]{:S(2)}) copy-start(bf16[4,128,2016]{2,1,0:T(8,128)(2,1)} %get-tuple-element.13) | copy-start | bytes 6193156
  83.9 1.0 %copy-start.1 = (bf16[4,128,504]{2,1,0:T(8,128)(2,1)S(1)}, bf16[4,128,504]{2,1,0:T(8,128)(2,1)}, u32[]{:S(2)}) copy-start(bf16[4,128,504]{2,1,0:T(8,128)(2,1)} %get-tuple-element.12) | copy-start | bytes 1548292
  84.9 1.0 %copy-start.2 = (bf16[4,128,384]{2,1,0:T(8,128)(2,1)S(1)}, bf16[4,128,384]{2,1,0:T(8,128)(2,1)}, u32[]{:S(2)}) copy-start(bf16[4,128,384]{2,1,0:T(8,128)(2,1)} %get-tuple-element.11) | copy-start | bytes 1179652

commit v4 on v3

--- a/solution.py
+++ b/solution.py
@@ -103,7 +103,7 @@
     )(tile_blocks, states, couplings)
 
 
-def gradient_kernel(blocks, states, lead_probs, tail_probs, grad, left):
+def gradient_kernel(blocks, states, lead_probs, tail_probs, probs, grad, turned, left):
     step = pl.program_id(0)
     rows, share = lead_probs.shape
     columns = tail_probs.shape[1]
@@ -125,6 +125,7 @@
         lead_gap = lead_probs[...].astype(jnp.float32).T - lead_table
         left[:, :rows] = lead_gap.astype(jnp.bfloat16)
         left[:, rows:] = lead_table.astype(jnp.bfloat16)
+        turned[...] = probs[...].astype(jnp.float32).T.astype(jnp.bfloat16)
 
     start = step * columns
     residue = residue_of(lax.broadcasted_iota(jnp.int32, (lanes, columns), 1) + start)
@@ -149,22 +150,29 @@
     grad[...] = jnp.where(own == other, 0.0, total * (Q / math.sqrt(rows)))
 
 
-def gradient(tile_blocks, states, lead_probs, tail_probs):
+def gradient(tile_blocks, states, lead_probs, tail_probs, probs):
     rows, share = lead_probs.shape
     return pl.pallas_call(
         gradient_kernel,
         grid=(pl.cdiv(WIDTH, COLUMN_TILE),),
-        out_shape=jax.ShapeDtypeStruct((share, WIDTH), jnp.float32),
+        out_shape=[
+            jax.ShapeDtypeStruct((share, WIDTH), jnp.float32),
+            jax.ShapeDtypeStruct(probs.shape[::-1], jnp.bfloat16),
+        ],
         in_specs=[
             pl.BlockSpec(memory_space=pltpu.SMEM),
             pl.BlockSpec(states.shape, lambda i: (0, 0)),
             pl.BlockSpec((rows, share), lambda i: (0, 0)),
             pl.BlockSpec((rows, COLUMN_TILE), lambda i: (0, i)),
-        ],
-        out_specs=pl.BlockSpec((share, COLUMN_TILE), lambda i: (0, i)),
+            pl.BlockSpec(probs.shape, lambda i: (0, 0)),
+        ],
+        out_specs=[
+            pl.BlockSpec((share, COLUMN_TILE), lambda i: (0, i)),
+            pl.BlockSpec(probs.shape[::-1], lambda i: (0, 0)),
+        ],
         scratch_shapes=[pltpu.VMEM((share, 2 * rows), jnp.bfloat16)],
-        compiler_params=pltpu.CompilerParams(vmem_limit_bytes=40 << 20),
-    )(tile_blocks, states, lead_probs, tail_probs)
+        compiler_params=pltpu.CompilerParams(vmem_limit_bytes=60 << 20),
+    )(tile_blocks, states, lead_probs, tail_probs, probs)
 
 
 def send(src, dst, send_sem, recv_sem, **device):
@@ -413,13 +421,14 @@
     probs, tail_probs, lead_probs, all_states = exchange(
         tile_blocks, lead, tail, states, fields[None, :], groups, seqs
     )
-    grad = gradient(
+    grad, turned = gradient(
         tile_blocks,
         all_states.reshape(row_total, states.shape[1]),
         lead_probs.reshape(row_total, share),
         tail_probs.reshape(row_total, WIDTH),
-    )
-    return (probs, grad[None])
+        probs,
+    )
+    return (turned.T, grad[None])
 
 
 def solution(mesh):

time: 93.2 us -> 88.8 us (0.953)
  local copies, waits for them, and re-layouts: 5.45 us -> 0 us
  Pallas kernels: 86.6 us -> 87.7 us
    unnamed x9 -> x0, local copies, waits for them, and re-layouts: 5.45 us -> none
    pallas_call x1, Pallas kernels: 6.8 us -> 7.9 us  [gradient(): pl.pallas_call(gradient_kernel, grid=(pl.cdiv(WIDTH, COLUMN_TILE),), out_...]
where the time goes in v4:
time: 88.8 us; the launch traced here: 88.4 us
  Pallas kernels  87.7 us (99%)
    pallas_call x1, Pallas kernels, exchange(): pl.pallas_call(functools.partial(exchange_kernel, groups, seqs), out_shap...  70.2 us
    pallas_call x1, Pallas kernels, tile_fields(): pl.pallas_call(field_kernel, grid=(WIDTH // ROW_TILE,), out_shape=[jax.Sh...  9.62 us
    pallas_call x1, Pallas kernels, gradient(): pl.pallas_call(gradient_kernel, grid=(pl.cdiv(WIDTH, COLUMN_TILE),), out_...  7.9 us

profile of v4, /device:TPU:28, one launch (start us, length us, event | category | flops | bytes accessed | tf_op | source)
XLA Modules:
  0.0 88.4 jit_solution(15000062367888985441)
XLA Ops:
  0.6 9.6 %shard_map.59 = (f32[6,128,336]{2,1,0:T(8,128)}, f32[128,2016]{1,0:T(8,128)}) custom-call(s32[1,2]{1,0:T(1,128)} %blocks.5, s32[128,384]{1,0:T(8,128)} %codes.3, bf16[1,2016,2016]{2,1,0:T(8,128)(2,1)} %weights.1), custom_call_target="tpu_custom_call" | custom-call | tf_op jit(solution)/shard_map/pallas_call | solution.py:82
  10.2 70.2 %shard_map.60 = (bf16[128,1008]{1,0:T(8,128)(2,1)}, bf16[4,128,2016]{2,1,0:T(8,128)(2,1)}, bf16[4,128,504]{2,1,0:T(8,128)(2,1)}, bf16[4,128,384]{2,1,0:T(8,128)(2,1)}) custom-call(s32[1,2]{1,0:T(1,128)} %blocks.5, f32[6,128,336]{2,1,0:T(8,128)} %get-tuple-element.10.lead, f32[128,2016]{1,0:T(8,128)} %get-tuple-element.11.tail, s32[128,384]{1,0:T(8,128)} %codes.3, ...), custom_call_target="tpu_custom_call" | custom-call | tf_op jit(solution)/shard_map/pallas_call | solution.py:382
  80.5 7.9 %shard_map.61 = (f32[504,2016]{1,0:T(8,128)}, bf16[1008,128]{1,0:T(8,128)(2,1)}) custom-call(s32[1,2]{1,0:T(1,128)} %blocks.5, bf16[512,384]{1,0:T(8,128)(2,1)} %bitcast.8, bf16[512,504]{1,0:T(8,128)(2,1)} %bitcast.7, bf16[512,2016]{1,0:T(8,128)(2,1)} %bitcast.6, bf16[128,1008]{1,0:T(8,128)(2,1)} %get-tuple-element.15.probs), custom_call_target="tpu_custom_call" | custom-call | tf_op jit(solution)/shard_map/pallas_call | solution.py:155
